TPU v7x, 32 devices: a whole 2x2x4 slice. The times are simulated.
32 devices in a mesh: seq: 8 (over z, x), head: 4 (over y, core).
Axes of the slice: x: 2, y: 2, z: 4, core: 2. Of those that a mesh axis runs over, the one named last changes fastest.
Arguments:
- projections: bfloat16 [4096, 3, 4096], P('seq', None, 'head'), may hold values from -53 to 53
- output_gradient: bfloat16 [4096, 5120], P('seq', 'head'), may hold values from -0.75 to 0.75
- output_projection_weight: bfloat16 [5120, 4096], P(None, 'head'), may hold values from -0.625 to 0.625
- kept_token_indices: int32 [8, 192], P('seq'), may hold values from -1 to 511, as said below
- surviving_token_count: int32 [8], replicated, may hold values from 64 to 192, as said below
Outputs:
- projection_grad: bfloat16 [4096, 3, 4096], P('seq', None, 'head')
- weight_grad: float32 [5120, 4096], P('seq', 'head')
Inputs may be any that keep to these rules, and one draw needn't show every extreme that they name: `kept_token_indices`: row s holds, in its first surviving_token_count[s] entries, distinct indices 0 to 511 in ascending order; its other entries are -1. Every shard that keeps 192 tokens keeps its last token. `surviving_token_count`: some shard keeps exactly 192 tokens and some other keeps exactly 64.
All inputs are finite; a program needn't handle non-finite values.
Results may differ from a plain program's by a relative error of at most 0.0099.
Values may be sent and summed in bfloat16 or wider, within the bound.
No kernel may reach another device: no remote copies, remote signals or barrier semaphores. Data moves between devices by JAX's collectives and lax.ppermute only.
A program may use at most 128 MiB of HBM per device.

v0:
```python
import functools
import math

import jax
import jax.numpy as jnp
from jax import lax
from jax.experimental import pallas as pl
from jax.experimental.pallas import tpu as pltpu
from jax.sharding import PartitionSpec as P

DH = 128
QUERY_BLOCK = 256
VMEM_BYTES = 48 * 1024 * 1024
F32 = jnp.float32
BF16 = jnp.bfloat16


def params():
    return pltpu.CompilerParams(vmem_limit_bytes=VMEM_BYTES)


def dot(left, right):
    return jnp.dot(left, right, preferred_element_type=F32)


def dot_rows(left, right):
    return lax.dot_general(left, right, (((0,), (0,)), ((), ())), preferred_element_type=F32)


def dot_cols(left, right):
    return lax.dot_general(left, right, (((1,), (1,)), ((), ())), preferred_element_type=F32)


def token_selector(index_ref, tokens):
    slots = index_ref.shape[1]
    token = lax.broadcasted_iota(jnp.int32, (tokens, slots), 0)
    return jnp.where(token == index_ref[...], 1.0, 0.0).astype(BF16)


def pack_grad_kernel(index_ref, grad_ref, out_ref):
    selector = token_selector(index_ref, grad_ref.shape[0])
    out_ref[...] = dot_rows(selector, grad_ref[...]).astype(BF16)


def pack_grad(index, grad):
    slots = index.shape[1]
    return pl.pallas_call(
        pack_grad_kernel,
        out_shape=jax.ShapeDtypeStruct((slots, grad.shape[1]), BF16),
        compiler_params=params(),
    )(index, grad)


def pack_heads_kernel(index_ref, proj_ref, out_ref):
    selector = token_selector(index_ref, proj_ref.shape[1])
    for which in range(3):
        rows = dot_rows(selector, proj_ref[which]).astype(BF16)
        for head in range(out_ref.shape[0]):
            out_ref[head, :, which * DH : (which + 1) * DH] = rows[:, head * DH : (head + 1) * DH]


def pack_heads(index, proj):
    slots = index.shape[1]
    _, tokens, width = proj.shape
    heads = width // DH
    step = 2
    return pl.pallas_call(
        pack_heads_kernel,
        grid=(heads // step,),
        in_specs=[
            pl.BlockSpec((1, slots), lambda i: (0, 0)),
            pl.BlockSpec((3, tokens, step * DH), lambda i: (0, 0, i)),
        ],
        out_specs=pl.BlockSpec((step, slots, 3 * DH), lambda i: (i, 0, 0)),
        out_shape=jax.ShapeDtypeStruct((heads, slots, 3 * DH), BF16),
        compiler_params=params(),
    )(index, proj)


def unpack_heads_kernel(index_ref, rows_ref, out_ref):
    selector = token_selector(index_ref, out_ref.shape[1])
    for head in range(rows_ref.shape[0]):
        tokens = dot(selector, rows_ref[head]).astype(BF16)
        for which in range(3):
            out_ref[which, :, head * DH : (head + 1) * DH] = tokens[
                :, which * DH : (which + 1) * DH
            ]


def unpack_heads(index, rows, tokens):
    heads, slots, _ = rows.shape
    step = 2
    return pl.pallas_call(
        unpack_heads_kernel,
        grid=(heads // step,),
        in_specs=[
            pl.BlockSpec((1, slots), lambda i: (0, 0)),
            pl.BlockSpec((step, slots, 3 * DH), lambda i: (i, 0, 0)),
        ],
        out_specs=pl.BlockSpec((3, tokens, step * DH), lambda i: (0, 0, i)),
        out_shape=jax.ShapeDtypeStruct((3, tokens, heads * DH), BF16),
        compiler_params=params(),
    )(index, rows)


def grad_attn_kernel(rows_ref, weight_ref, out_ref):
    product = dot(rows_ref[...], weight_ref[...]).astype(BF16)
    for head in range(out_ref.shape[0]):
        out_ref[head] = product[:, head * DH : (head + 1) * DH]


def grad_attn_heads(rows, weight):
    slots, depth = rows.shape
    heads = weight.shape[1] // DH
    step = 2
    return pl.pallas_call(
        grad_attn_kernel,
        grid=(heads // step,),
        in_specs=[
            pl.BlockSpec((slots, depth), lambda i: (0, 0)),
            pl.BlockSpec((depth, step * DH), lambda i: (0, i)),
        ],
        out_specs=pl.BlockSpec((step, slots, DH), lambda i: (i, 0, 0)),
        out_shape=jax.ShapeDtypeStruct((heads, slots, DH), BF16),
        compiler_params=params(),
    )(rows, weight)


def weight_grad_kernel(rows_ref, attended_ref, out_ref):
    attended = jnp.concatenate([attended_ref[head] for head in range(attended_ref.shape[0])], axis=1)
    out_ref[...] = dot_rows(rows_ref[...], attended)


def weight_grad_heads(rows, attended):
    total, width = rows.shape
    heads = attended.shape[0]
    step = 2
    return pl.pallas_call(
        weight_grad_kernel,
        grid=(heads // step,),
        in_specs=[
            pl.BlockSpec((total, width), lambda i: (0, 0)),
            pl.BlockSpec((step, total, DH), lambda i: (i, 0, 0)),
        ],
        out_specs=pl.BlockSpec((width, step * DH), lambda i: (0, i)),
        out_shape=jax.ShapeDtypeStruct((width, heads * DH), F32),
        compiler_params=params(),
    )(rows, attended)


def attention_kernel(
    slots,
    part_rows,
    part_ref,
    live_ref,
    query_ref,
    grad_ref,
    key_ref,
    value_ref,
    attended_ref,
    query_grad_ref,
    key_grad_ref,
    value_grad_ref,
    key_total,
    value_total,
):
    scale = 1.0 / math.sqrt(DH)
    rows_total = query_ref.shape[0]
    keys_total = key_ref.shape[0]
    quarters = slots // part_rows
    key_flip = key_ref[...].T
    value_flip = value_ref[...].T
    for start in range(0, rows_total, QUERY_BLOCK):
        rows = slice(start, start + QUERY_BLOCK)
        last = start + QUERY_BLOCK - 1
        last_pos = last // part_rows * slots + (quarters - 1) * part_rows + last % part_rows
        first_pos = start // part_rows * slots + start % part_rows
        keys = min(-(-(last_pos + 1) // 128) * 128, keys_total)
        clear = first_pos // 128 * 128
        query = query_ref[rows]
        grad = grad_ref[rows]
        row = start + lax.broadcasted_iota(jnp.int32, (1, QUERY_BLOCK), 1)
        if quarters > 1:
            shard = row // part_rows
            row = shard * slots + part_ref[0] * part_rows + row - shard * part_rows
        scores = dot_cols(key_ref[:keys], query) * scale + live_ref[:keys, :1]
        key_pos = clear + lax.broadcasted_iota(jnp.int32, (keys - clear, 1), 0)
        edge = jnp.where(key_pos <= row, scores[clear:], -1e30)
        scores = jnp.concatenate([scores[:clear], edge], axis=0) if clear else edge
        peak = jnp.max(scores, axis=0, keepdims=True)
        weights = jnp.exp(scores - peak)
        probs = weights * (1.0 / jnp.sum(weights, axis=0, keepdims=True))
        probs_low = probs.astype(BF16)
        attended = dot(value_flip[:, :keys], probs_low)
        attended_ref[rows] = attended.T.astype(BF16)
        row_dot = jnp.sum(grad.T.astype(F32) * attended, axis=0, keepdims=True)
        grad_probs = dot_cols(value_ref[:keys], grad)
        grad_scores = (probs * (grad_probs - row_dot)).astype(BF16)
        query_grad = dot(key_flip[:, :keys], grad_scores) * scale
        query_grad_ref[rows] = query_grad.T.astype(BF16)
        key_part = dot(grad_scores, query)
        value_part = dot(probs_low, grad)
        prev = start - 1
        reached = 0
        if start:
            prev_pos = prev // part_rows * slots + (quarters - 1) * part_rows + prev % part_rows
            reached = min(-(-(prev_pos + 1) // 128) * 128, keys_total)
        if reached:
            key_total[:reached] += key_part[:reached]
            value_total[:reached] += value_part[:reached]
        if keys > reached:
            key_total[reached:keys] = key_part[reached:]
            value_total[reached:keys] = value_part[reached:]
    key_grad_ref[...] = (key_total[...] * scale).astype(key_grad_ref.dtype)
    value_grad_ref[...] = value_total[...].astype(value_grad_ref.dtype)


def attention(part, live, query, grad, key, value, slots, part_rows, key_type):
    rows, keys = query.shape[0], key.shape[0]
    vmem = pl.BlockSpec(memory_space=pltpu.VMEM)
    return pl.pallas_call(
        functools.partial(attention_kernel, slots, part_rows),
        in_specs=[pl.BlockSpec(memory_space=pltpu.SMEM)] + [vmem] * 5,
        out_specs=[vmem] * 4,
        out_shape=[
            jax.ShapeDtypeStruct((rows, DH), BF16),
            jax.ShapeDtypeStruct((rows, DH), BF16),
            jax.ShapeDtypeStruct((keys, DH), key_type),
            jax.ShapeDtypeStruct((keys, DH), key_type),
        ],
        scratch_shapes=[pltpu.VMEM((keys, DH), F32)] * 2,
        compiler_params=params(),
    )(part, live, query, grad, key, value)


def on_device_split_heads(
    projections,
    output_gradient,
    output_projection_weight,
    kept_token_indices,
    surviving_token_count,
):
    tok_dev = projections.shape[0]
    group_width = projections.shape[2]
    slots = kept_token_indices.shape[1]
    heads = group_width // DH
    seq_count = lax.axis_size("seq")
    head_count = lax.axis_size("head")
    quarters = seq_count // heads
    part_rows = slots // quarters
    part = (lax.axis_index("seq") % quarters).astype(jnp.int32).reshape(1)
    index = kept_token_indices
    keys = seq_count * slots

    grad_local = pack_grad(index, output_gradient)
    grad_rows = lax.all_gather(grad_local, "head", axis=1, tiled=True)
    packed = pack_heads(index, projections.transpose(1, 0, 2))

    position = jnp.arange(slots, dtype=jnp.int32)
    live = position[None, :] < surviving_token_count[:, None]
    live = jnp.where(live, 0.0, -1e30).astype(F32).reshape(keys, 1)
    live = jnp.broadcast_to(live, (keys, DH))

    def swap(blocks):
        return lax.all_to_all(blocks, "seq", split_axis=0, concat_axis=0, tiled=True)

    if quarters == 1:
        arrived = swap(packed).reshape(keys, 3 * DH)
        query, key, value = (arrived[:, n * DH : (n + 1) * DH] for n in range(3))
    else:
        query = swap(packed[:, :, :DH].reshape(seq_count, part_rows, DH))
        query = query.reshape(seq_count * part_rows, DH)
        sides = jnp.broadcast_to(packed[:, None, :, DH:], (heads, quarters, slots, 2 * DH))
        sides = swap(sides.reshape(seq_count, slots, 2 * DH)).reshape(keys, 2 * DH)
        key, value = sides[:, :DH], sides[:, DH:]

    grad_heads = grad_attn_heads(grad_rows, output_projection_weight)
    grad_in = swap(grad_heads.reshape(seq_count, part_rows, DH)).reshape(-1, DH)

    width = grad_rows.shape[1] // seq_count
    piece = slots // head_count
    mine = lax.dynamic_slice_in_dim(grad_rows, lax.axis_index("head") * piece, piece, 0)
    mine = swap(mine.reshape(piece, seq_count, width).transpose(1, 0, 2))
    all_rows = lax.all_gather(mine, "head", axis=1, tiled=True)

    key_type = BF16 if quarters == 1 else F32
    attended, query_grad, key_grad, value_grad = attention(
        part, live, query, grad_in, key, value, slots, part_rows, key_type
    )

    gathered = lax.all_gather(attended, "seq", axis=0).reshape(heads, keys, DH)
    all_rows = all_rows.reshape(seq_count, quarters, part_rows, width).transpose(1, 0, 2, 3)
    weight_grad = weight_grad_heads(all_rows.reshape(keys, width), gathered)

    if quarters == 1:
        back = jnp.concatenate([query_grad, key_grad, value_grad], axis=1)
        home = swap(back.reshape(seq_count, slots, 3 * DH))
    else:
        query_home = swap(query_grad.reshape(seq_count, part_rows, DH)).reshape(heads, slots, DH)
        back = jnp.concatenate([key_grad, value_grad], axis=1)
        key_home = swap(back.reshape(seq_count, slots, 2 * DH))
        key_home = jnp.sum(key_home.reshape(heads, quarters, slots, 2 * DH), axis=1)
        home = jnp.concatenate([query_home, key_home.astype(BF16)], axis=2)
    projection_grad = unpack_heads(index, home, tok_dev).transpose(1, 0, 2)
    return (projection_grad, weight_grad)


def gather_blocks(block, axis, bits):
    count = lax.axis_size(axis)
    held = {0: block}
    for bit in bits:
        pairs = [(i, i ^ bit) for i in range(count)]
        held.update({step ^ bit: lax.ppermute(held[step], axis, pairs) for step in list(held)})
    return [held[step] for step in range(count)]


SMEM_SPEC = pl.BlockSpec(memory_space=pltpu.SMEM)
VMEM_SPEC = pl.BlockSpec(memory_space=pltpu.VMEM)


def grad_swap_kernel(count, place_ref, *refs):
    row_refs, weight_ref, out_ref, total = refs[:count], refs[count], refs[count + 1], refs[count + 2]
    mine = place_ref[1]
    seq_count, height, _ = out_ref.shape
    slots, depth = row_refs[0].shape
    piece = slots // count
    chunks = (height - slots) // piece
    per_block = depth // (chunks * DH)
    for step in range(count):

        @pl.when(pl.program_id(0) == step)
        def _(step=step):
            part = dot(row_refs[step][...], weight_ref[...])
            total[...] = part if step == 0 else total[...] + part
            share = row_refs[step][pl.ds(pl.multiple_of(mine * piece, piece), piece), :]
            for chunk in range(per_block * chunks):
                partner = (mine ^ step) * per_block + chunk // chunks
                start = slots + chunk % chunks * piece
                out_ref[partner, start : start + piece, :] = share[:, chunk * DH : (chunk + 1) * DH]

    @pl.when(pl.program_id(0) == count - 1)
    def _():
        for head in range(seq_count):
            out_ref[head, :slots, :] = total[:, head * DH : (head + 1) * DH].astype(BF16)


def grad_swap(place, blocks, weight, seq_count):
    count = len(blocks)
    slots, depth = blocks[0].shape
    columns = weight.shape[1]
    height = slots + slots // count * (count * depth // seq_count // DH)
    return pl.pallas_call(
        functools.partial(grad_swap_kernel, count),
        grid_spec=pltpu.PrefetchScalarGridSpec(
            num_scalar_prefetch=1,
            grid=(count,),
            in_specs=[pl.BlockSpec((slots, depth), lambda i, place: (0, 0))] * count
            + [pl.BlockSpec((depth, columns), lambda i, place: (place[1] ^ i, 0))],
            out_specs=pl.BlockSpec((seq_count, height, DH), lambda i, place: (0, 0, 0)),
            scratch_shapes=[pltpu.VMEM((slots, columns), F32)],
        ),
        out_shape=jax.ShapeDtypeStruct((seq_count, height, DH), BF16),
        compiler_params=params(),
        cost_estimate=pl.CostEstimate(
            flops=2 * slots * count * depth * columns,
            bytes_accessed=2 * count * depth * columns,
            transcendentals=0,
        ),
    )(place, *blocks, weight)


def weight_grad_swap_kernel(head_count, seq_count, place_ref, *refs):
    piece_refs = refs[:head_count]
    attended_refs = refs[head_count : head_count + seq_count]
    out_ref, rows = refs[-2:]
    me, mine = place_ref[0], place_ref[1]
    chunks = rows.shape[1] // DH
    piece = piece_refs[0].shape[1] // chunks
    slots = piece * head_count
    for part in range(head_count):
        for shard in range(seq_count):
            here = pl.ds(pl.multiple_of(shard * slots + (mine ^ part) * piece, piece), piece)
            for chunk in range(chunks):
                rows[here, chunk * DH : (chunk + 1) * DH] = piece_refs[part][
                    shard, chunk * piece : (chunk + 1) * piece, :
                ]
    for step in range(0, seq_count, 2):
        pair = jnp.concatenate([attended_refs[step][...], attended_refs[step + 1][...]], axis=1)
        product = dot_rows(rows[...], pair)
        for side in range(2):
            column = pl.multiple_of((me ^ (step + side)) * DH, DH)
            out_ref[:, pl.ds(column, DH)] = product[:, side * DH : (side + 1) * DH]


def weight_grad_swap(place, pieces, attended):
    head_count, seq_count = len(pieces), len(attended)
    keys = attended[0].shape[0]
    width = pieces[0].shape[1] // (keys // seq_count // head_count) * DH
    return pl.pallas_call(
        functools.partial(weight_grad_swap_kernel, head_count, seq_count),
        in_specs=[SMEM_SPEC] + [VMEM_SPEC] * (head_count + seq_count),
        out_specs=VMEM_SPEC,
        out_shape=jax.ShapeDtypeStruct((width, seq_count * DH), F32),
        scratch_shapes=[pltpu.VMEM((keys, width), BF16)],
        compiler_params=params(),
        cost_estimate=pl.CostEstimate(
            flops=2 * keys * width * seq_count * DH,
            bytes_accessed=8 * keys * DH * seq_count,
            transcendentals=0,
        ),
    )(place, *pieces, *attended)


def masked_scores(start, keys, key_ref, query, live_ref):
    scores = dot_cols(key_ref[:keys], query) * (1.0 / math.sqrt(DH)) + live_ref[:keys, :1]
    row = start + lax.broadcasted_iota(jnp.int32, (1, QUERY_BLOCK), 1)
    key_pos = start + lax.broadcasted_iota(jnp.int32, (QUERY_BLOCK, 1), 0)
    edge = jnp.where(key_pos <= row, scores[start:], -1e30)
    return jnp.concatenate([scores[:start], edge], axis=0) if start else edge


def forward_kernel(
    live_ref, block_ref, attended_ref, query_ref, key_ref, value_ref, flip_ref, stat_ref
):
    seq_count, slots, _ = block_ref.shape
    for shard in range(seq_count):
        here = slice(shard * slots, (shard + 1) * slots)
        for which, ref in enumerate((query_ref, key_ref, value_ref)):
            ref[here] = block_ref[shard, :, which * DH : (which + 1) * DH]
    value_flip = value_ref[...].T
    for start in range(0, query_ref.shape[0], QUERY_BLOCK):
        rows = slice(start, start + QUERY_BLOCK)
        keys = start + QUERY_BLOCK
        scores = masked_scores(start, keys, key_ref, query_ref[rows], live_ref)
        peak = jnp.max(scores, axis=0, keepdims=True)
        weights = jnp.exp(scores - peak)
        inverse = 1.0 / jnp.sum(weights, axis=0, keepdims=True)
        attended = dot(value_flip[:, :keys], (weights * inverse).astype(BF16))
        attended_ref[rows] = attended.T.astype(BF16)
        flip_ref[:, rows] = attended
        stat_ref[0:1, rows] = peak
        stat_ref[1:2, rows] = inverse


def attention_cost(keys, dots):
    return pl.CostEstimate(
        flops=dots * keys * keys * DH, bytes_accessed=16 * keys * DH, transcendentals=keys * keys // 2
    )


def forward(live, blocks):
    keys = blocks.shape[0] * blocks.shape[1]
    rows = jax.ShapeDtypeStruct((keys, DH), BF16)
    return pl.pallas_call(
        forward_kernel,
        in_specs=[VMEM_SPEC] * 2,
        out_specs=[VMEM_SPEC] * 6,
        out_shape=[rows] * 4
        + [jax.ShapeDtypeStruct((DH, keys), F32), jax.ShapeDtypeStruct((8, keys), F32)],
        compiler_params=params(),
        cost_estimate=attention_cost(keys, 2),
    )(live, blocks)


def backward_kernel(
    live_ref,
    query_ref,
    key_ref,
    value_ref,
    flip_ref,
    stat_ref,
    grads_ref,
    out_ref,
    grad_ref,
    query_total,
    key_total,
    value_total,
):
    seq_count, slots, _ = out_ref.shape
    scale = 1.0 / math.sqrt(DH)
    for shard in range(seq_count):
        grad_ref[shard * slots : (shard + 1) * slots] = grads_ref[shard, :slots]
    key_flip = key_ref[...].T
    for start in range(0, query_ref.shape[0], QUERY_BLOCK):
        rows = slice(start, start + QUERY_BLOCK)
        keys = start + QUERY_BLOCK
        query = query_ref[rows]
        grad = grad_ref[rows]
        scores = masked_scores(start, keys, key_ref, query, live_ref)
        probs = jnp.exp(scores - stat_ref[0:1, rows]) * stat_ref[1:2, rows]
        probs_low = probs.astype(BF16)
        row_dot = jnp.sum(grad.T.astype(F32) * flip_ref[:, rows], axis=0, keepdims=True)
        grad_probs = dot_cols(value_ref[:keys], grad)
        grad_scores = (probs * (grad_probs - row_dot)).astype(BF16)
        query_total[rows] = (dot(key_flip[:, :keys], grad_scores) * scale).T.astype(BF16)
        key_part = dot(grad_scores, query)
        value_part = dot(probs_low, grad)
        if start:
            key_total[:start] += key_part[:start]
            value_total[:start] += value_part[:start]
        key_total[rows] = key_part[start:]
        value_total[rows] = value_part[start:]
    for shard in range(seq_count):
        here = slice(shard * slots, (shard + 1) * slots)
        out_ref[shard, :, :DH] = query_total[here]
        out_ref[shard, :, DH : 2 * DH] = (key_total[here] * scale).astype(BF16)
        out_ref[shard, :, 2 * DH :] = value_total[here].astype(BF16)


def backward(live, query, key, value, flip, stats, grads):
    seq_count = grads.shape[0]
    keys = query.shape[0]
    return pl.pallas_call(
        backward_kernel,
        in_specs=[VMEM_SPEC] * 7,
        out_specs=VMEM_SPEC,
        out_shape=jax.ShapeDtypeStruct((seq_count, keys // seq_count, 3 * DH), BF16),
        scratch_shapes=[pltpu.VMEM((keys, DH), BF16)] * 2 + [pltpu.VMEM((keys, DH), F32)] * 2,
        compiler_params=params(),
        cost_estimate=attention_cost(keys, 5),
    )(live, query, key, value, flip, stats, grads)


def live_bias(counts, slots):
    position = jnp.arange(slots, dtype=jnp.int32)
    live = position[None, :] < counts[:, None]
    live = jnp.where(live, 0.0, -1e30).astype(F32).reshape(-1, 1)
    return jnp.broadcast_to(live, (live.shape[0], DH))


def on_device_whole_heads(
    projections,
    output_gradient,
    output_projection_weight,
    kept_token_indices,
    surviving_token_count,
):
    tok_dev = projections.shape[0]
    slots = kept_token_indices.shape[1]
    seq_count = lax.axis_size("seq")
    head_count = lax.axis_size("head")
    index = kept_token_indices
    place = jnp.stack([lax.axis_index("seq"), lax.axis_index("head")]).astype(jnp.int32)
    seq_bits = [1 << bit for bit in reversed(range(seq_count.bit_length() - 1))]
    head_bits = [1 << bit for bit in reversed(range(head_count.bit_length() - 1))]

    grad_local = pack_grad(index, output_gradient)
    grad_blocks = gather_blocks(grad_local, "head", head_bits)
    packed = pack_heads(index, projections.transpose(1, 0, 2))
    live = live_bias(surviving_token_count, slots)

    def swap(blocks):
        return lax.all_to_all(blocks, "seq", split_axis=0, concat_axis=0, tiled=True)

    arrived = swap(packed)
    grads = swap(grad_swap(place, grad_blocks, output_projection_weight, seq_count))
    attended, query, key, value, flip, stats = forward(live, arrived)
    gathered = gather_blocks(attended, "seq", seq_bits)
    pieces = gather_blocks(grads[:, slots:], "head", head_bits)
    home = swap(backward(live, query, key, value, flip, stats, grads))
    weight_grad = weight_grad_swap(place, pieces, gathered)
    projection_grad = unpack_heads(index, home, tok_dev).transpose(1, 0, 2)
    return (projection_grad, weight_grad)


def on_device(projections, output_gradient, weight, index, counts):
    heads = projections.shape[2] // DH
    seq_count, head_count = lax.axis_size("seq"), lax.axis_size("head")
    width = output_gradient.shape[1] * head_count // seq_count
    whole = seq_count == heads and seq_count % 2 == 0 and width % DH == 0
    powers = seq_count & (seq_count - 1) == 0 and head_count & (head_count - 1) == 0
    body = on_device_whole_heads if whole and powers else on_device_split_heads
    return body(projections, output_gradient, weight, index, counts)


def solution(mesh):
    return jax.shard_map(
        on_device,
        mesh=mesh,
        in_specs=(P("seq", None, "head"), P("seq", "head"), P(None, "head"), P("seq", None), P()),
        out_specs=(P("seq", None, "head"), P("seq", "head")),
        check_vma=False,
    )
```

profile of v0, /device:TPU:0, one launch (start us, length us, event | category | flops | bytes accessed | tf_op | source)
XLA Modules:
  0.0 164.2 jit_solution(10587595493396117504)
XLA Ops:
  0.6 1.9 %copy-done = bf16[512,3,1024]{2,0,1:T(8,128)(2,1)S(1)} copy-done((bf16[512,3,1024]{2,0,1:T(8,128)(2,1)S(1)}, bf16[512,3,1024]{2,0,1:T(8,128)(2,1)}, u32[]{:S(2)}) %copy-start) | copy-done | bytes 3145752
  3.2 2.9 %shard_map.68 = bf16[8,192,384]{2,1,0:T(8,128)(2,1)} custom-call(s32[1,192]{1,0:T(1,128)S(1)} %copy-done.4, bf16[3,512,1024]{2,1,0:T(8,128)(2,1)S(1)} %bitcast.4), custom_call_target="tpu_custom_call" | custom-call | tf_op jit(solution)/shard_map/pallas_call | solution.py:67
  6.1 7.4 %all-to-all-start = ((bf16[8,192,384]{2,1,0:T(8,128)(2,1)}), bf16[8,192,384]{2,1,0:T(8,128)(2,1)S(1)}, u32[]{:S(2)}, u32[]{:S(2)}) async-start(bf16[8,192,384]{2,1,0:T(8,128)(2,1)} %shard_map.68), calls=%async_computation | async-start | bytes 2359296 | tf_op jit(solution)/shard_map/all_to_all | solution.py:553
  14.0 1.6 collective-permute-start.1
  15.6 11.2 %collective-permute-done.1.refs_2_ = bf16[192,1280]{1,0:T(8,128)(2,1)S(1)} collective-permute-done((bf16[192,1280]{1,0:T(8,128)(2,1)S(1)}, bf16[192,1280]{1,0:T(8,128)(2,1)S(1)}, u32[]{:S(2)}, u32[]{:S(2)}) %collective-permute-start.1) | collective-permute-done | bytes 491552 | tf_op jit(solution)/shard_map/ppermute | solution.py:313
  26.8 1.8 %collective-permute-done.2.refs_3_ = bf16[192,1280]{1,0:T(8,128)(2,1)S(1)} collective-permute-done((bf16[192,1280]{1,0:T(8,128)(2,1)S(1)}, bf16[192,1280]{1,0:T(8,128)(2,1)S(1)}, u32[]{:S(2)}, u32[]{:S(2)}) %collective-permute-start.2) | collective-permute-done | bytes 491552 | tf_op jit(solution)/shard_map/ppermute | solution.py:313
  28.6 7.3 %shard_map.71 = bf16[8,432,128]{2,1,0:T(8,128)(2,1)} custom-call(s32[2]{0:T(128)S(1)} %pad_add_fusion.place_ref, bf16[192,1280]{1,0:T(8,128)(2,1)S(1)} %shard_map.70.refs_0_, bf16[192,1280]{1,0:T(8,128)(2,1)S(1)} %collective-permute-done.refs_1_, bf16[192,1280]{1,0:T(8,128)(2,1)S(1)} %collective-permute-done.1.refs_2_, ...), custom_call_target="tpu_custom_call" | custom-call | flops 2013265920 | bytes 10485760 | tf_op jit(solution)/shard_map/pallas_call | solution.py:352
  35.9 6.1 %all-to-all-done.block_ref = bf16[8,192,384]{2,1,0:T(8,128)(2,1)S(1)} async-done(((bf16[8,192,384]{2,1,0:T(8,128)(2,1)}), bf16[8,192,384]{2,1,0:T(8,128)(2,1)S(1)}, u32[]{:S(2)}, u32[]{:S(2)}) %all-to-all-start) | async-done | bytes 1179680 | tf_op jit(solution)/shard_map/all_to_all | solution.py:553
  42.1 3.6 %all-to-all-start.1 = ((bf16[8,432,128]{2,1,0:T(8,128)(2,1)}), bf16[8,432,128]{2,1,0:T(8,128)(2,1)S(1)}, u32[]{:S(2)}, u32[]{:S(2)}) async-start(bf16[8,432,128]{2,1,0:T(8,128)(2,1)} %shard_map.71), calls=%async_computation.1 | async-start | bytes 1769472 | tf_op jit(solution)/shard_map/all_to_all | solution.py:553
  46.1 4.5 %shard_map.69 = (bf16[1536,128]{1,0:T(8,128)(2,1)S(1)}, bf16[1536,128]{1,0:T(8,128)(2,1)S(1)}, bf16[1536,128]{1,0:T(8,128)(2,1)S(1)}, bf16[1536,128]{1,0:T(8,128...) custom-call(f32[1536,128]{1,0:T(8,128)S(1)} %broadcast_in_dim.17.live_ref, ...), custom_call_target="tpu_custom_call" | custom-call | flops 603979776 | bytes 3145728 | tf_op jit(solution)/shard_map/pallas_call | solution.py:454
  53.8 14.3 %all-to-all-done.1.grads_ref = bf16[8,432,128]{2,1,0:T(8,128)(2,1)S(1)} async-done(((bf16[8,432,128]{2,1,0:T(8,128)(2,1)}), bf16[8,432,128]{2,1,0:T(8,128)(2,1)S(1)}, u32[]{:S(2)}, u32[]{:S(2)}) %all-to-all-start.1) | async-done | bytes 884768 | tf_op jit(solution)/shard_map/all_to_all | solution.py:553
  72.3 5.2 %shard_map.72 = bf16[8,192,384]{2,1,0:T(8,128)(2,1)} custom-call(f32[1536,128]{1,0:T(8,128)S(1)} %broadcast_in_dim.17.live_ref, bf16[1536,128]{1,0:T(8,128)(2,1)S(1)} %copy-done.9, bf16[1536,128]{1,0:T(8,128)(2,1)S(1)} %copy-done.11, bf16[1536,128]{1,0:T(8,128)(2,1)S(1)} %copy-done.13, f32[128,1536]{1,0:T(8,128)S(1)} %copy-done.7, ...), custom_call_target="tpu_custom_call" | custom-call | flops 1509949440 | bytes 3145728 | tf_op jit(solution)/shard_map/pallas_call | solution.py:513
  77.5 3.7 %all-to-all-start.2 = ((bf16[8,192,384]{2,1,0:T(8,128)(2,1)}), bf16[8,192,384]{2,1,0:T(8,128)(2,1)S(1)}, u32[]{:S(2)}, u32[]{:S(2)}) async-start(bf16[8,192,384]{2,1,0:T(8,128)(2,1)} %shard_map.72), calls=%async_computation.2 | async-start | bytes 2359296 | tf_op jit(solution)/shard_map/all_to_all | solution.py:553
  81.3 2.8 %collective-permute-start.9 = (bf16[1536,128]{1,0:T(8,128)(2,1)}, bf16[1536,128]{1,0:T(8,128)(2,1)S(1)}, u32[]{:S(2)}, u32[]{:S(2)}) collective-permute-start(bf16[1536,128]{1,0:T(8,128)(2,1)} %copy-done.2), channel_id=1, source_target_pairs={{0,16},{4,20},{8,24},{12,28},{16,0},{20,4},{24,8},{28,12},{1,17},{... | collective-permute-start | bytes 1179656 | tf_op jit(solution)/shard_map/ppermute | solution.py:313
  84.0 1.6 collective-permute-start.4
  85.6 1.5 collective-permute-start.7
  87.1 1.5 collective-permute-start.6
  88.5 38.2 %collective-permute-done.9.refs_8_ = bf16[1536,128]{1,0:T(8,128)(2,1)S(1)} collective-permute-done((bf16[1536,128]{1,0:T(8,128)(2,1)}, bf16[1536,128]{1,0:T(8,128)(2,1)S(1)}, u32[]{:S(2)}, u32[]{:S(2)}) %collective-permute-start.9) | collective-permute-done | bytes 393248 | tf_op jit(solution)/shard_map/ppermute | solution.py:313
  129.3 7.4 %collective-permute-done.11.refs_10_ = bf16[1536,128]{1,0:T(8,128)(2,1)S(1)} collective-permute-done((bf16[1536,128]{1,0:T(8,128)(2,1)S(1)}, bf16[1536,128]{1,0:T(8,128)(2,1)S(1)}, u32[]{:S(2)}, u32[]{:S(2)}) %collective-permute-start.11) | collective-permute-done | bytes 393248 | tf_op jit(solution)/shard_map/ppermute | solution.py:313
  136.7 1.6 collective-permute-start.12
  139.2 8.4 %collective-permute-done.8.refs_7_ = bf16[1536,128]{1,0:T(8,128)(2,1)S(1)} collective-permute-done((bf16[1536,128]{1,0:T(8,128)(2,1)S(1)}, bf16[1536,128]{1,0:T(8,128)(2,1)S(1)}, u32[]{:S(2)}, u32[]{:S(2)}) %collective-permute-start.8) | collective-permute-done | bytes 393248 | tf_op jit(solution)/shard_map/ppermute | solution.py:313
  147.7 7.5 %collective-permute-done.12.refs_11_ = bf16[1536,128]{1,0:T(8,128)(2,1)S(1)} collective-permute-done((bf16[1536,128]{1,0:T(8,128)(2,1)S(1)}, bf16[1536,128]{1,0:T(8,128)(2,1)S(1)}, u32[]{:S(2)}, u32[]{:S(2)}) %collective-permute-start.12) | collective-permute-done | bytes 393248 | tf_op jit(solution)/shard_map/ppermute | solution.py:313
  156.2 4.9 %shard_map.74 = f32[640,1024]{1,0:T(8,128)} custom-call(s32[2]{0:T(128)S(1)} %pad_add_fusion.place_ref, bf16[8,240,128]{2,1,0:T(8,128)(2,1)S(1)} %slice.4.refs_0_, bf16[8,240,128]{2,1,0:T(8,128)(2,1)S(1)} %collective-permute-done.3.refs_1_, bf16[8,240,128]{2,1,0:T(8,128)(2,1)S(1)} %collective-permute-done.4.refs_2_, ...), custom_call_target="tpu_custom_call" | custom-call | flops 2013265920 | bytes 12582912 | tf_op jit(solution)/shard_map/pallas_call | solution.py:399
  161.1 3.1 %shard_map.73 = bf16[3,512,1024]{2,1,0:T(8,128)(2,1)} custom-call(s32[1,192]{1,0:T(1,128)S(1)} %copy-done.5, bf16[8,192,384]{2,1,0:T(8,128)(2,1)S(1)} %all-to-all-done.2.rows_ref), custom_call_target="tpu_custom_call" | custom-call | tf_op jit(solution)/shard_map/pallas_call | solution.py:93
  (50 shorter events, 13.5 us)
Async XLA Ops:
  0.6 1.9 %copy-start = (bf16[512,3,1024]{2,0,1:T(8,128)(2,1)S(1)}, bf16[512,3,1024]{2,0,1:T(8,128)(2,1)}, u32[]{:S(2)}) copy-start(bf16[512,3,1024]{2,0,1:T(8,128)(2,1)} %param.5) | copy-start | bytes 9437188
  6.1 7.4 %copy-start.1 = (bf16[512,1280]{1,0:T(8,128)(2,1)S(1)}, bf16[512,1280]{1,0:T(8,128)(2,1)}, u32[]{:S(2)}) copy-start(bf16[512,1280]{1,0:T(8,128)(2,1)} %grad_ref.1) | copy-start | bytes 3932164
  6.1 7.4 %copy-start.5 = (s32[1,192]{1,0:T(1,128)S(1)}, s32[1,192]{1,0:T(1,128)}, u32[]{:S(2)}) copy-start(s32[1,192]{1,0:T(1,128)} %index_ref.5) | copy-start | bytes 2308
  6.1 36.0 %all-to-all-start = ((bf16[8,192,384]{2,1,0:T(8,128)(2,1)}), bf16[8,192,384]{2,1,0:T(8,128)(2,1)S(1)}, u32[]{:S(2)}, u32[]{:S(2)}) async-start(bf16[8,192,384]{2,1,0:T(8,128)(2,1)} %shard_map.68), calls=%async_computation | async-start | bytes 2359296 | tf_op jit(solution)/shard_map/all_to_all | solution.py:553
  14.0 12.7 %collective-permute-start.1 = (bf16[192,1280]{1,0:T(8,128)(2,1)S(1)}, bf16[192,1280]{1,0:T(8,128)(2,1)S(1)}, u32[]{:S(2)}, u32[]{:S(2)}) collective-permute-start(bf16[192,1280]{1,0:T(8,128)(2,1)S(1)} %shard_map.70.refs_0_), channel_id=1, source_target_pairs={{0,2},{1,3},{2,0},{3,1},{4,6},{5,7},{6,4},{7,5},{8,10},{9,11},{10,... | collective-permute-start | bytes 1474568 | tf_op jit(solution)/shard_map/ppermute | solution.py:313
  15.6 11.2 %collective-permute-start = (bf16[192,1280]{1,0:T(8,128)(2,1)S(1)}, bf16[192,1280]{1,0:T(8,128)(2,1)S(1)}, u32[]{:S(2)}, u32[]{:S(2)}) collective-permute-start(bf16[192,1280]{1,0:T(8,128)(2,1)S(1)} %shard_map.70.refs_0_), channel_id=1, source_target_pairs={{0,1},{1,0},{2,3},{3,2},{4,5},{5,4},{6,7},{7,6},{8,9},{9,8},{10,11... | collective-permute-start | bytes 1474568 | tf_op jit(solution)/shard_map/ppermute | solution.py:313
  26.7 1.9 %collective-permute-start.2 = (bf16[192,1280]{1,0:T(8,128)(2,1)S(1)}, bf16[192,1280]{1,0:T(8,128)(2,1)S(1)}, u32[]{:S(2)}, u32[]{:S(2)}) collective-permute-start(bf16[192,1280]{1,0:T(8,128)(2,1)S(1)} %collective-permute-done.1.refs_2_), channel_id=1, source_target_pairs={{0,1},{1,0},{2,3},{3,2},{4,5},{5,4},{6,7},{7,6},{8,9},{9,8},{10,11... | collective-permute-start | bytes 1474568 | tf_op jit(solution)/shard_map/ppermute | solution.py:313
  35.9 9.8 %copy-start.14 = (s32[8]{0:T(128)S(1)}, s32[8]{0:T(128)}, u32[]{:S(2)}) copy-start(s32[8]{0:T(128)} %param.9) | copy-start | bytes 100
  42.1 26.1 %all-to-all-start.1 = ((bf16[8,432,128]{2,1,0:T(8,128)(2,1)}), bf16[8,432,128]{2,1,0:T(8,128)(2,1)S(1)}, u32[]{:S(2)}, u32[]{:S(2)}) async-start(bf16[8,432,128]{2,1,0:T(8,128)(2,1)} %shard_map.71), calls=%async_computation.1 | async-start | bytes 1769472 | tf_op jit(solution)/shard_map/all_to_all | solution.py:553
  53.8 23.7 %copy-start.2 = (bf16[1536,128]{1,0:T(8,128)(2,1)}, bf16[1536,128]{1,0:T(8,128)(2,1)S(1)}, u32[]{:S(2)}) copy-start(bf16[1536,128]{1,0:T(8,128)(2,1)S(1)} %get-tuple-element.13.refs_4_) | copy-start | bytes 1179652
  68.1 1.1 copy-start.7
  69.3 1.0 copy-start.9
  77.5 83.6 %all-to-all-start.2 = ((bf16[8,192,384]{2,1,0:T(8,128)(2,1)}), bf16[8,192,384]{2,1,0:T(8,128)(2,1)S(1)}, u32[]{:S(2)}, u32[]{:S(2)}) async-start(bf16[8,192,384]{2,1,0:T(8,128)(2,1)} %shard_map.72), calls=%async_computation.2 | async-start | bytes 2359296 | tf_op jit(solution)/shard_map/all_to_all | solution.py:553
  81.3 45.5 %collective-permute-start.9 = (bf16[1536,128]{1,0:T(8,128)(2,1)}, bf16[1536,128]{1,0:T(8,128)(2,1)S(1)}, u32[]{:S(2)}, u32[]{:S(2)}) collective-permute-start(bf16[1536,128]{1,0:T(8,128)(2,1)} %copy-done.2), channel_id=1, source_target_pairs={{0,16},{4,20},{8,24},{12,28},{16,0},{20,4},{24,8},{28,12},{1,17},{... | collective-permute-start | bytes 1179656 | tf_op jit(solution)/shard_map/ppermute | solution.py:313
  84.0 42.7 %collective-permute-start.4 = (bf16[8,240,128]{2,1,0:T(8,128)(2,1)S(1)}, bf16[8,240,128]{2,1,0:T(8,128)(2,1)S(1)}, u32[]{:S(2)}, u32[]{:S(2)}) collective-permute-start(bf16[8,240,128]{2,1,0:T(8,128)(2,1)S(1)} %slice.4.refs_0_), channel_id=1, source_target_pairs={{0,2},{1,3},{2,0},{3,1},{4,6},{5,7},{6,4},{7,5},{8,10},{9,11},{10,... | collective-permute-start | bytes 1474568 | tf_op jit(solution)/shard_map/ppermute | solution.py:313
  85.6 41.7 %collective-permute-start.7 = (bf16[1536,128]{1,0:T(8,128)(2,1)}, bf16[1536,128]{1,0:T(8,128)(2,1)S(1)}, u32[]{:S(2)}, u32[]{:S(2)}) collective-permute-start(bf16[1536,128]{1,0:T(8,128)(2,1)} %copy-done.2), channel_id=1, source_target_pairs={{0,8},{4,12},{8,0},{12,4},{16,24},{20,28},{24,16},{28,20},{1,9},{5... | collective-permute-start | bytes 1179656 | tf_op jit(solution)/shard_map/ppermute | solution.py:313
  87.1 41.6 %collective-permute-start.6 = (bf16[1536,128]{1,0:T(8,128)(2,1)}, bf16[1536,128]{1,0:T(8,128)(2,1)S(1)}, u32[]{:S(2)}, u32[]{:S(2)}) collective-permute-start(bf16[1536,128]{1,0:T(8,128)(2,1)} %copy-done.2), channel_id=1, source_target_pairs={{0,4},{4,0},{8,12},{12,8},{16,20},{20,16},{24,28},{28,24},{1,5},{5... | collective-permute-start | bytes 1179656 | tf_op jit(solution)/shard_map/ppermute | solution.py:313
  126.7 9.9 %collective-permute-start.11 = (bf16[1536,128]{1,0:T(8,128)(2,1)S(1)}, bf16[1536,128]{1,0:T(8,128)(2,1)S(1)}, u32[]{:S(2)}, u32[]{:S(2)}) collective-permute-start(bf16[1536,128]{1,0:T(8,128)(2,1)S(1)} %collective-permute-done.9.refs_8_), channel_id=1, source_target_pairs={{0,8},{4,12},{8,0},{12,4},{16,24},{20,28},{24,16},{28,20},{1,9},{5... | collective-permute-start | bytes 1179656 | tf_op jit(solution)/shard_map/ppermute | solution.py:313
  126.8 20.9 %collective-permute-start.3 = (bf16[8,240,128]{2,1,0:T(8,128)(2,1)S(1)}, bf16[8,240,128]{2,1,0:T(8,128)(2,1)S(1)}, u32[]{:S(2)}, u32[]{:S(2)}) collective-permute-start(bf16[8,240,128]{2,1,0:T(8,128)(2,1)S(1)} %slice.4.refs_0_), channel_id=1, source_target_pairs={{0,1},{1,0},{2,3},{3,2},{4,5},{5,4},{6,7},{7,6},{8,9},{9,8},{10,11... | collective-permute-start | bytes 1474568 | tf_op jit(solution)/shard_map/ppermute | solution.py:313
  126.8 28.5 %collective-permute-start.5 = (bf16[8,240,128]{2,1,0:T(8,128)(2,1)S(1)}, bf16[8,240,128]{2,1,0:T(8,128)(2,1)S(1)}, u32[]{:S(2)}, u32[]{:S(2)}) collective-permute-start(bf16[8,240,128]{2,1,0:T(8,128)(2,1)S(1)} %collective-permute-done.4.refs_2_), channel_id=1, source_target_pairs={{0,1},{1,0},{2,3},{3,2},{4,5},{5,4},{6,7},{7,6},{8,9},{9,8},{10,11... | collective-permute-start | bytes 1474568 | tf_op jit(solution)/shard_map/ppermute | solution.py:313
  127.3 12.0 %collective-permute-start.10 = (bf16[1536,128]{1,0:T(8,128)(2,1)S(1)}, bf16[1536,128]{1,0:T(8,128)(2,1)S(1)}, u32[]{:S(2)}, u32[]{:S(2)}) collective-permute-start(bf16[1536,128]{1,0:T(8,128)(2,1)S(1)} %collective-permute-done.9.refs_8_), channel_id=1, source_target_pairs={{0,4},{4,0},{8,12},{12,8},{16,20},{20,16},{24,28},{28,24},{1,5},{5... | collective-permute-start | bytes 1179656 | tf_op jit(solution)/shard_map/ppermute | solution.py:313
  128.6 19.0 %collective-permute-start.8 = (bf16[1536,128]{1,0:T(8,128)(2,1)S(1)}, bf16[1536,128]{1,0:T(8,128)(2,1)S(1)}, u32[]{:S(2)}, u32[]{:S(2)}) collective-permute-start(bf16[1536,128]{1,0:T(8,128)(2,1)S(1)} %collective-permute-done.7.refs_6_), channel_id=1, source_target_pairs={{0,4},{4,0},{8,12},{12,8},{16,20},{20,16},{24,28},{28,24},{1,5},{5... | collective-permute-start | bytes 1179656 | tf_op jit(solution)/shard_map/ppermute | solution.py:313
  136.7 18.5 %collective-permute-start.12 = (bf16[1536,128]{1,0:T(8,128)(2,1)S(1)}, bf16[1536,128]{1,0:T(8,128)(2,1)S(1)}, u32[]{:S(2)}, u32[]{:S(2)}) collective-permute-start(bf16[1536,128]{1,0:T(8,128)(2,1)S(1)} %collective-permute-done.11.refs_10_), channel_id=1, source_target_pairs={{0,4},{4,0},{8,12},{12,8},{16,20},{20,16},{24,28},{28,24},{1,5},{5... | collective-permute-start | bytes 1179656 | tf_op jit(solution)/shard_map/ppermute | solution.py:313
  155.2 1.0 copy-start.3
  (7 other events, 5.8 us)
where the time goes:
time: 165 us; the launch traced here: 164 us
  waiting for transfers between devices  96 us (58%)
  Pallas kernels  28.4 us (17%)
  starting transfers between devices  27.7 us (17%)
  local copies, waits for them, and re-layouts  11.2 us (7%)
    ppermute x13, waiting for transfers between devices, gather_blocks(): lax.ppermute(held[step], axis, pairs)  75.5 us
    all_to_all x3, waiting for transfers between devices, swap(): lax.all_to_all(blocks, 'seq', split_axis=0, concat_axis=0, tiled=True)  20.5 us
    all_to_all x3, starting transfers between devices, swap(): lax.all_to_all(blocks, 'seq', split_axis=0, concat_axis=0, tiled=True)  14.8 us
    ppermute x13, starting transfers between devices, gather_blocks(): lax.ppermute(held[step], axis, pairs)  12.9 us
    unnamed x30, local copies, waits for them, and re-layouts  10.8 us
    pallas_call x1, Pallas kernels, grad_swap(): pl.pallas_call(functools.partial(grad_swap_kernel, count), grid_spec=pltp...  7.33 us
    pallas_call x1, Pallas kernels, backward(): pl.pallas_call(backward_kernel, in_specs=[VMEM_SPEC] * 7, out_specs=VMEM_...  5.23 us
    pallas_call x1, Pallas kernels, weight_grad_swap(): pl.pallas_call(functools.partial(weight_grad_swap_kernel, head_count, seq...  4.88 us
  transfers between devices with their start and end apart: 16, of which 9 were waited for; matrix products, arithmetic and copies ran while one was open for 0% of the time, Pallas kernels for 10%

commit v1 on v0

--- a/solution.py
+++ b/solution.py
@@ -10,7 +10,7 @@
 
 DH = 128
 QUERY_BLOCK = 256
-VMEM_BYTES = 48 * 1024 * 1024
+VMEM_BYTES = 20 * 1024 * 1024
 F32 = jnp.float32
 BF16 = jnp.bfloat16
 
@@ -305,13 +305,19 @@
     return (projection_grad, weight_grad)
 
 
-def gather_blocks(block, axis, bits):
-    count = lax.axis_size(axis)
+def exchange(block, axis, bit):
+    return lax.ppermute(block, axis, [(i, i ^ bit) for i in range(lax.axis_size(axis))])
+
+
+def gather_blocks(block, axis, bits, first=None):
     held = {0: block}
     for bit in bits:
-        pairs = [(i, i ^ bit) for i in range(count)]
-        held.update({step ^ bit: lax.ppermute(held[step], axis, pairs) for step in list(held)})
-    return [held[step] for step in range(count)]
+        for step in list(held):
+            if first is not None and step == 0:
+                held[bit] = first[bit]
+            else:
+                held[step ^ bit] = exchange(held[step], axis, bit)
+    return [held[step] for step in range(lax.axis_size(axis))]
 
 
 SMEM_SPEC = pl.BlockSpec(memory_space=pltpu.SMEM)
@@ -555,9 +561,12 @@
     arrived = swap(packed)
     grads = swap(grad_swap(place, grad_blocks, output_projection_weight, seq_count))
     attended, query, key, value, flip, stats = forward(live, arrived)
-    gathered = gather_blocks(attended, "seq", seq_bits)
+    first = {bit: exchange(attended, "seq", bit) for bit in seq_bits}
     pieces = gather_blocks(grads[:, slots:], "head", head_bits)
-    home = swap(backward(live, query, key, value, flip, stats, grads))
+    back = backward(live, query, key, value, flip, stats, grads)
+    back, first = lax.optimization_barrier((back, first))
+    home = swap(back)
+    gathered = gather_blocks(attended, "seq", seq_bits, first)
     weight_grad = weight_grad_swap(place, pieces, gathered)
     projection_grad = unpack_heads(index, home, tok_dev).transpose(1, 0, 2)
     return (projection_grad, weight_grad)

time: 165 us -> 144 us (0.87)
  waiting for transfers between devices: 96 us -> 72.7 us
  local copies, waits for them, and re-layouts: 11.2 us -> 14.2 us
  Pallas kernels: 28.4 us -> 25.9 us
    ppermute x13, waiting for transfers between devices: 75.5 us -> 49.4 us  [exchange(): lax.ppermute(block, axis, [(i, i ^ bit) for i in range(lax.axis_size(axis...]
    unnamed x30 -> x32, local copies, waits for them, and re-layouts: 10.8 us -> 13.8 us
    pallas_call x1, Pallas kernels: 7.33 us -> 4.37 us  [grad_swap(): pl.pallas_call(functools.partial(grad_swap_kernel, count), grid_spec=pltp...]
    all_to_all x3, waiting for transfers between devices: 20.5 us -> 23.2 us  [swap(): lax.all_to_all(blocks, 'seq', split_axis=0, concat_axis=0, tiled=True)]
  transfers between devices with their start and end apart: 16 -> 16, of which waited for: 9 -> 8; matrix products, arithmetic and copies ran while one was open for 0% -> 0% of each run, Pallas kernels for 10% -> 14%
where the time goes in v1:
time: 144 us; the launch traced here: 143 us
  waiting for transfers between devices  72.7 us (50%)
  starting transfers between devices  29.3 us (20%)
  Pallas kernels  25.9 us (18%)
  local copies, waits for them, and re-layouts  14.2 us (10%)
    ppermute x13, waiting for transfers between devices, exchange(): lax.ppermute(block, axis, [(i, i ^ bit) for i in range(lax.axis_size(axis...  49.4 us
    all_to_all x3, waiting for transfers between devices, swap(): lax.all_to_all(blocks, 'seq', split_axis=0, concat_axis=0, tiled=True)  23.2 us
    all_to_all x3, starting transfers between devices, swap(): lax.all_to_all(blocks, 'seq', split_axis=0, concat_axis=0, tiled=True)  14.9 us
    ppermute x13, starting transfers between devices, exchange(): lax.ppermute(block, axis, [(i, i ^ bit) for i in range(lax.axis_size(axis...  14.3 us
    unnamed x32, local copies, waits for them, and re-layouts  13.8 us
    pallas_call x1, Pallas kernels, weight_grad_swap(): pl.pallas_call(functools.partial(weight_grad_swap_kernel, head_count, seq...  5.33 us
    pallas_call x1, Pallas kernels, backward(): pl.pallas_call(backward_kernel, in_specs=[VMEM_SPEC] * 7, out_specs=VMEM_...  5.24 us
    pallas_call x1, Pallas kernels, forward(): pl.pallas_call(forward_kernel, in_specs=[VMEM_SPEC] * 2, out_specs=[VMEM_...  4.53 us
  transfers between devices with their start and end apart: 16, of which 8 were waited for; matrix products, arithmetic and copies ran while one was open for 0% of the time, Pallas kernels for 14%

profile of v1, /device:TPU:0, one launch (start us, length us, event | category | flops | bytes accessed | tf_op | source)
XLA Modules:
  0.0 142.9 jit_solution(6269161855010128094)
XLA Ops:
  0.6 1.9 %copy-done.1 = bf16[512,3,1024]{2,0,1:T(8,128)(2,1)S(1)} copy-done((bf16[512,3,1024]{2,0,1:T(8,128)(2,1)S(1)}, bf16[512,3,1024]{2,0,1:T(8,128)(2,1)}, u32[]{:S(2)}) %copy-start.1) | copy-done | bytes 3145752
  3.2 2.9 %shard_map.68 = bf16[8,192,384]{2,1,0:T(8,128)(2,1)} custom-call(s32[1,192]{1,0:T(1,128)S(1)} %copy-done.5, bf16[3,512,1024]{2,1,0:T(8,128)(2,1)S(1)} %bitcast.4), custom_call_target="tpu_custom_call" | custom-call | tf_op jit(solution)/shard_map/pallas_call | solution.py:67
  6.1 7.4 %all-to-all-start = ((bf16[8,192,384]{2,1,0:T(8,128)(2,1)}), bf16[8,192,384]{2,1,0:T(8,128)(2,1)S(1)}, u32[]{:S(2)}, u32[]{:S(2)}) async-start(bf16[8,192,384]{2,1,0:T(8,128)(2,1)} %shard_map.68), calls=%async_computation | async-start | bytes 2359296 | tf_op jit(solution)/shard_map/all_to_all | solution.py:559
  14.0 1.6 %collective-permute-start.1 = (bf16[192,1280]{1,0:T(8,128)(2,1)S(1)}, bf16[192,1280]{1,0:T(8,128)(2,1)S(1)}, u32[]{:S(2)}, u32[]{:S(2)}) collective-permute-start(bf16[192,1280]{1,0:T(8,128)(2,1)S(1)} %shard_map.70.refs_0_), channel_id=1, source_target_pairs={{0,2},{1,3},{2,0},{3,1},{4,6},{5,7},{6,4},{7,5},{8,10},{9,11},{10,... | collective-permute-start | bytes 1474568 | tf_op jit(solution)/shard_map/ppermute | solution.py:309
  15.6 11.2 %collective-permute-done.1.refs_2_ = bf16[192,1280]{1,0:T(8,128)(2,1)S(1)} collective-permute-done((bf16[192,1280]{1,0:T(8,128)(2,1)S(1)}, bf16[192,1280]{1,0:T(8,128)(2,1)S(1)}, u32[]{:S(2)}, u32[]{:S(2)}) %collective-permute-start.1) | collective-permute-done | bytes 491552 | tf_op jit(solution)/shard_map/ppermute | solution.py:309
  26.8 1.8 %collective-permute-done.2.refs_3_ = bf16[192,1280]{1,0:T(8,128)(2,1)S(1)} collective-permute-done((bf16[192,1280]{1,0:T(8,128)(2,1)S(1)}, bf16[192,1280]{1,0:T(8,128)(2,1)S(1)}, u32[]{:S(2)}, u32[]{:S(2)}) %collective-permute-start.2) | collective-permute-done | bytes 491552 | tf_op jit(solution)/shard_map/ppermute | solution.py:309
  28.6 4.0 %copy-done = bf16[5120,1024]{1,0:T(8,128)(2,1)S(1)} copy-done((bf16[5120,1024]{1,0:T(8,128)(2,1)S(1)}, bf16[5120,1024]{1,0:T(8,128)(2,1)}, u32[]{:S(2)}) %copy-start) | copy-done | bytes 10485784
  32.6 4.4 %shard_map.71 = bf16[8,432,128]{2,1,0:T(8,128)(2,1)} custom-call(s32[2]{0:T(128)S(1)} %pad_add_fusion.place_ref, bf16[192,1280]{1,0:T(8,128)(2,1)S(1)} %shard_map.70.refs_0_, bf16[192,1280]{1,0:T(8,128)(2,1)S(1)} %collective-permute-done.refs_1_, bf16[192,1280]{1,0:T(8,128)(2,1)S(1)} %collective-permute-done.1.refs_2_, ...), custom_call_target="tpu_custom_call" | custom-call | flops 2013265920 | bytes 10485760 | tf_op jit(solution)/shard_map/pallas_call | solution.py:358
  36.9 5.1 %all-to-all-done.block_ref = bf16[8,192,384]{2,1,0:T(8,128)(2,1)S(1)} async-done(((bf16[8,192,384]{2,1,0:T(8,128)(2,1)}), bf16[8,192,384]{2,1,0:T(8,128)(2,1)S(1)}, u32[]{:S(2)}, u32[]{:S(2)}) %all-to-all-start) | async-done | bytes 1179680 | tf_op jit(solution)/shard_map/all_to_all | solution.py:559
  42.1 3.6 %all-to-all-start.1 = ((bf16[8,432,128]{2,1,0:T(8,128)(2,1)}), bf16[8,432,128]{2,1,0:T(8,128)(2,1)S(1)}, u32[]{:S(2)}, u32[]{:S(2)}) async-start(bf16[8,432,128]{2,1,0:T(8,128)(2,1)} %shard_map.71), calls=%async_computation.1 | async-start | bytes 1769472 | tf_op jit(solution)/shard_map/all_to_all | solution.py:559
  46.1 4.5 %shard_map.69 = (bf16[1536,128]{1,0:T(8,128)(2,1)S(1)}, bf16[1536,128]{1,0:T(8,128)(2,1)S(1)}, bf16[1536,128]{1,0:T(8,128)(2,1)S(1)}, bf16[1536,128]{1,0:T(8,128...) custom-call(f32[1536,128]{1,0:T(8,128)S(1)} %broadcast_in_dim.17.live_ref, ...), custom_call_target="tpu_custom_call" | custom-call | flops 603979776 | bytes 3145728 | tf_op jit(solution)/shard_map/pallas_call | solution.py:460
  53.8 2.9 %collective-permute-start.5 = (bf16[1536,128]{1,0:T(8,128)(2,1)S(1)}, bf16[1536,128]{1,0:T(8,128)(2,1)S(1)}, u32[]{:S(2)}, u32[]{:S(2)}) collective-permute-start(bf16[1536,128]{1,0:T(8,128)(2,1)S(1)} %get-tuple-element.17.refs_4_), channel_id=1, source_target_pairs={{0,16},{4,20},{8,24},{12,28},{16,0},{20,4},{24,8},{28,12},{1,17},{... | collective-permute-start | bytes 1179656 | tf_op jit(solution)/shard_map/ppermute | solution.py:309
  59.7 18.1 %all-to-all-done.1.grads_ref = bf16[8,432,128]{2,1,0:T(8,128)(2,1)S(1)} async-done(((bf16[8,432,128]{2,1,0:T(8,128)(2,1)}), bf16[8,432,128]{2,1,0:T(8,128)(2,1)S(1)}, u32[]{:S(2)}, u32[]{:S(2)}) %all-to-all-start.1) | async-done | bytes 884768 | tf_op jit(solution)/shard_map/all_to_all | solution.py:559
  81.9 5.2 %shard_map.72 = bf16[8,192,384]{2,1,0:T(8,128)(2,1)} custom-call(f32[1536,128]{1,0:T(8,128)S(1)} %broadcast_in_dim.17.live_ref, bf16[1536,128]{1,0:T(8,128)(2,1)S(1)} %copy-done.10, bf16[1536,128]{1,0:T(8,128)(2,1)S(1)} %copy-done.12, bf16[1536,128]{1,0:T(8,128)(2,1)S(1)} %copy-done.14, f32[128,1536]{1,0:T(8,128)S(1)} %copy-done.8, ...), custom_call_target="tpu_custom_call" | custom-call | flops 1509949440 | bytes 3145728 | tf_op jit(solution)/shard_map/pallas_call | solution.py:519
  87.2 3.9 %all-to-all-start.2 = ((bf16[8,192,384]{2,1,0:T(8,128)(2,1)}), bf16[8,192,384]{2,1,0:T(8,128)(2,1)S(1)}, u32[]{:S(2)}, u32[]{:S(2)}) async-start(bf16[8,192,384]{2,1,0:T(8,128)(2,1)} %shard_map.72), calls=%async_computation.2 | async-start | bytes 2359296 | tf_op jit(solution)/shard_map/all_to_all | solution.py:559
  91.1 1.6 %collective-permute-start.7 = (bf16[8,240,128]{2,1,0:T(8,128)(2,1)S(1)}, bf16[8,240,128]{2,1,0:T(8,128)(2,1)S(1)}, u32[]{:S(2)}, u32[]{:S(2)}) collective-permute-start(bf16[8,240,128]{2,1,0:T(8,128)(2,1)S(1)} %slice.4.refs_0_), channel_id=1, source_target_pairs={{0,2},{1,3},{2,0},{3,1},{4,6},{5,7},{6,4},{7,5},{8,10},{9,11},{10,... | collective-permute-start | bytes 1474568 | tf_op jit(solution)/shard_map/ppermute | solution.py:309
  92.7 1.9 %collective-permute-start.11 = (bf16[1536,128]{1,0:T(8,128)(2,1)S(1)}, bf16[1536,128]{1,0:T(8,128)(2,1)S(1)}, u32[]{:S(2)}, u32[]{:S(2)}) collective-permute-start(bf16[1536,128]{1,0:T(8,128)(2,1)S(1)} %collective-permute-done.5.refs_8_), channel_id=1, source_target_pairs={{0,8},{4,12},{8,0},{12,4},{16,24},{20,28},{24,16},{28,20},{1,9},{5... | collective-permute-start | bytes 1179656 | tf_op jit(solution)/shard_map/ppermute | solution.py:309
  94.6 8.1 %collective-permute-done.7.refs_2_ = bf16[8,240,128]{2,1,0:T(8,128)(2,1)S(1)} collective-permute-done((bf16[8,240,128]{2,1,0:T(8,128)(2,1)S(1)}, bf16[8,240,128]{2,1,0:T(8,128)(2,1)S(1)}, u32[]{:S(2)}, u32[]{:S(2)}) %collective-permute-start.7) | collective-permute-done | bytes 491552 | tf_op jit(solution)/shard_map/ppermute | solution.py:309
  102.7 1.7 %collective-permute-start.9 = (bf16[1536,128]{1,0:T(8,128)(2,1)S(1)}, bf16[1536,128]{1,0:T(8,128)(2,1)S(1)}, u32[]{:S(2)}, u32[]{:S(2)}) collective-permute-start(bf16[1536,128]{1,0:T(8,128)(2,1)S(1)} %collective-permute-done.4.refs_6_), channel_id=1, source_target_pairs={{0,4},{4,0},{8,12},{12,8},{16,20},{20,16},{24,28},{28,24},{1,5},{5... | collective-permute-start | bytes 1179656 | tf_op jit(solution)/shard_map/ppermute | solution.py:309
  104.7 15.0 %collective-permute-done.11.refs_10_ = bf16[1536,128]{1,0:T(8,128)(2,1)S(1)} collective-permute-done((bf16[1536,128]{1,0:T(8,128)(2,1)S(1)}, bf16[1536,128]{1,0:T(8,128)(2,1)S(1)}, u32[]{:S(2)}, u32[]{:S(2)}) %collective-permute-start.11) | collective-permute-done | bytes 393248 | tf_op jit(solution)/shard_map/ppermute | solution.py:309
  121.1 5.2 %collective-permute-done.10.refs_9_ = bf16[1536,128]{1,0:T(8,128)(2,1)S(1)} collective-permute-done((bf16[1536,128]{1,0:T(8,128)(2,1)S(1)}, bf16[1536,128]{1,0:T(8,128)(2,1)S(1)}, u32[]{:S(2)}, u32[]{:S(2)}) %collective-permute-start.10) | collective-permute-done | bytes 393248 | tf_op jit(solution)/shard_map/ppermute | solution.py:309
  126.3 8.2 %collective-permute-done.12.refs_11_ = bf16[1536,128]{1,0:T(8,128)(2,1)S(1)} collective-permute-done((bf16[1536,128]{1,0:T(8,128)(2,1)S(1)}, bf16[1536,128]{1,0:T(8,128)(2,1)S(1)}, u32[]{:S(2)}, u32[]{:S(2)}) %collective-permute-start.12) | collective-permute-done | bytes 393248 | tf_op jit(solution)/shard_map/ppermute | solution.py:309
  134.5 5.3 %shard_map.74 = f32[640,1024]{1,0:T(8,128)} custom-call(s32[2]{0:T(128)S(1)} %pad_add_fusion.place_ref, bf16[8,240,128]{2,1,0:T(8,128)(2,1)S(1)} %slice.4.refs_0_, bf16[8,240,128]{2,1,0:T(8,128)(2,1)S(1)} %collective-permute-done.6.refs_1_, bf16[8,240,128]{2,1,0:T(8,128)(2,1)S(1)} %collective-permute-done.7.refs_2_, ...), custom_call_target="tpu_custom_call" | custom-call | flops 2013265920 | bytes 12582912 | tf_op jit(solution)/shard_map/pallas_call | solution.py:405
  139.8 3.1 %shard_map.73 = bf16[3,512,1024]{2,1,0:T(8,128)(2,1)} custom-call(s32[1,192]{1,0:T(1,128)S(1)} %copy-done.6, bf16[8,192,384]{2,1,0:T(8,128)(2,1)S(1)} %all-to-all-done.2.rows_ref), custom_call_target="tpu_custom_call" | custom-call | tf_op jit(solution)/shard_map/pallas_call | solution.py:93
  (52 shorter events, 13.6 us)
Async XLA Ops:
  0.6 1.9 %copy-start.1 = (bf16[512,3,1024]{2,0,1:T(8,128)(2,1)S(1)}, bf16[512,3,1024]{2,0,1:T(8,128)(2,1)}, u32[]{:S(2)}) copy-start(bf16[512,3,1024]{2,0,1:T(8,128)(2,1)} %param.5) | copy-start | bytes 9437188
  6.1 7.4 %copy-start.2 = (bf16[512,1280]{1,0:T(8,128)(2,1)S(1)}, bf16[512,1280]{1,0:T(8,128)(2,1)}, u32[]{:S(2)}) copy-start(bf16[512,1280]{1,0:T(8,128)(2,1)} %grad_ref.1) | copy-start | bytes 3932164
  6.1 7.4 %copy-start.6 = (s32[1,192]{1,0:T(1,128)S(1)}, s32[1,192]{1,0:T(1,128)}, u32[]{:S(2)}) copy-start(s32[1,192]{1,0:T(1,128)} %index_ref.5) | copy-start | bytes 2308
  6.1 36.0 %all-to-all-start = ((bf16[8,192,384]{2,1,0:T(8,128)(2,1)}), bf16[8,192,384]{2,1,0:T(8,128)(2,1)S(1)}, u32[]{:S(2)}, u32[]{:S(2)}) async-start(bf16[8,192,384]{2,1,0:T(8,128)(2,1)} %shard_map.68), calls=%async_computation | async-start | bytes 2359296 | tf_op jit(solution)/shard_map/all_to_all | solution.py:559
  14.0 12.7 %collective-permute-start.1 = (bf16[192,1280]{1,0:T(8,128)(2,1)S(1)}, bf16[192,1280]{1,0:T(8,128)(2,1)S(1)}, u32[]{:S(2)}, u32[]{:S(2)}) collective-permute-start(bf16[192,1280]{1,0:T(8,128)(2,1)S(1)} %shard_map.70.refs_0_), channel_id=1, source_target_pairs={{0,2},{1,3},{2,0},{3,1},{4,6},{5,7},{6,4},{7,5},{8,10},{9,11},{10,... | collective-permute-start | bytes 1474568 | tf_op jit(solution)/shard_map/ppermute | solution.py:309
  15.6 11.2 %collective-permute-start = (bf16[192,1280]{1,0:T(8,128)(2,1)S(1)}, bf16[192,1280]{1,0:T(8,128)(2,1)S(1)}, u32[]{:S(2)}, u32[]{:S(2)}) collective-permute-start(bf16[192,1280]{1,0:T(8,128)(2,1)S(1)} %shard_map.70.refs_0_), channel_id=1, source_target_pairs={{0,1},{1,0},{2,3},{3,2},{4,5},{5,4},{6,7},{7,6},{8,9},{9,8},{10,11... | collective-permute-start | bytes 1474568 | tf_op jit(solution)/shard_map/ppermute | solution.py:309
  26.7 1.9 %collective-permute-start.2 = (bf16[192,1280]{1,0:T(8,128)(2,1)S(1)}, bf16[192,1280]{1,0:T(8,128)(2,1)S(1)}, u32[]{:S(2)}, u32[]{:S(2)}) collective-permute-start(bf16[192,1280]{1,0:T(8,128)(2,1)S(1)} %collective-permute-done.1.refs_2_), channel_id=1, source_target_pairs={{0,1},{1,0},{2,3},{3,2},{4,5},{5,4},{6,7},{7,6},{8,9},{9,8},{10,11... | collective-permute-start | bytes 1474568 | tf_op jit(solution)/shard_map/ppermute | solution.py:309
  28.6 4.0 %copy-start = (bf16[5120,1024]{1,0:T(8,128)(2,1)S(1)}, bf16[5120,1024]{1,0:T(8,128)(2,1)}, u32[]{:S(2)}) copy-start(bf16[5120,1024]{1,0:T(8,128)(2,1)} %refs_4_.1) | copy-start | bytes 31457284
  36.9 8.8 %copy-start.15 = (s32[8]{0:T(128)S(1)}, s32[8]{0:T(128)}, u32[]{:S(2)}) copy-start(s32[8]{0:T(128)} %param.9) | copy-start | bytes 100
  42.1 35.7 %all-to-all-start.1 = ((bf16[8,432,128]{2,1,0:T(8,128)(2,1)}), bf16[8,432,128]{2,1,0:T(8,128)(2,1)S(1)}, u32[]{:S(2)}, u32[]{:S(2)}) async-start(bf16[8,432,128]{2,1,0:T(8,128)(2,1)} %shard_map.71), calls=%async_computation.1 | async-start | bytes 1769472 | tf_op jit(solution)/shard_map/all_to_all | solution.py:559
  53.8 33.3 %copy-start.3 = (bf16[1536,128]{1,0:T(8,128)(2,1)}, bf16[1536,128]{1,0:T(8,128)(2,1)S(1)}, u32[]{:S(2)}) copy-start(bf16[1536,128]{1,0:T(8,128)(2,1)S(1)} %get-tuple-element.17.refs_4_) | copy-start | bytes 1179652
  53.8 33.3 %collective-permute-start.5 = (bf16[1536,128]{1,0:T(8,128)(2,1)S(1)}, bf16[1536,128]{1,0:T(8,128)(2,1)S(1)}, u32[]{:S(2)}, u32[]{:S(2)}) collective-permute-start(bf16[1536,128]{1,0:T(8,128)(2,1)S(1)} %get-tuple-element.17.refs_4_), channel_id=1, source_target_pairs={{0,16},{4,20},{8,24},{12,28},{16,0},{20,4},{24,8},{28,12},{1,17},{... | collective-permute-start | bytes 1179656 | tf_op jit(solution)/shard_map/ppermute | solution.py:309
  56.7 30.4 %collective-permute-start.4 = (bf16[1536,128]{1,0:T(8,128)(2,1)S(1)}, bf16[1536,128]{1,0:T(8,128)(2,1)S(1)}, u32[]{:S(2)}, u32[]{:S(2)}) collective-permute-start(bf16[1536,128]{1,0:T(8,128)(2,1)S(1)} %get-tuple-element.17.refs_4_), channel_id=1, source_target_pairs={{0,8},{4,12},{8,0},{12,4},{16,24},{20,28},{24,16},{28,20},{1,9},{5... | collective-permute-start | bytes 1179656 | tf_op jit(solution)/shard_map/ppermute | solution.py:309
  58.2 29.0 %collective-permute-start.3 = (bf16[1536,128]{1,0:T(8,128)(2,1)S(1)}, bf16[1536,128]{1,0:T(8,128)(2,1)}, u32[]{:S(2)}, u32[]{:S(2)}) collective-permute-start(bf16[1536,128]{1,0:T(8,128)(2,1)S(1)} %get-tuple-element.17.refs_4_), channel_id=1, source_target_pairs={{0,4},{4,0},{8,12},{12,8},{16,20},{20,16},{24,28},{28,24},{1,5},{5... | collective-permute-start | bytes 1179656 | tf_op jit(solution)/shard_map/ppermute | solution.py:309
  77.8 1.1 copy-start.8
  87.1 47.3 %copy-start.4 = (bf16[1536,128]{1,0:T(8,128)(2,1)S(1)}, bf16[1536,128]{1,0:T(8,128)(2,1)}, u32[]{:S(2)}) copy-start(bf16[1536,128]{1,0:T(8,128)(2,1)} %copy-done.3) | copy-start | bytes 1179652
  87.2 52.7 %all-to-all-start.2 = ((bf16[8,192,384]{2,1,0:T(8,128)(2,1)}), bf16[8,192,384]{2,1,0:T(8,128)(2,1)S(1)}, u32[]{:S(2)}, u32[]{:S(2)}) async-start(bf16[8,192,384]{2,1,0:T(8,128)(2,1)} %shard_map.72), calls=%async_computation.2 | async-start | bytes 2359296 | tf_op jit(solution)/shard_map/all_to_all | solution.py:559
  91.1 11.5 %collective-permute-start.7 = (bf16[8,240,128]{2,1,0:T(8,128)(2,1)S(1)}, bf16[8,240,128]{2,1,0:T(8,128)(2,1)S(1)}, u32[]{:S(2)}, u32[]{:S(2)}) collective-permute-start(bf16[8,240,128]{2,1,0:T(8,128)(2,1)S(1)} %slice.4.refs_0_), channel_id=1, source_target_pairs={{0,2},{1,3},{2,0},{3,1},{4,6},{5,7},{6,4},{7,5},{8,10},{9,11},{10,... | collective-permute-start | bytes 1474568 | tf_op jit(solution)/shard_map/ppermute | solution.py:309
  92.7 27.0 %collective-permute-start.11 = (bf16[1536,128]{1,0:T(8,128)(2,1)S(1)}, bf16[1536,128]{1,0:T(8,128)(2,1)S(1)}, u32[]{:S(2)}, u32[]{:S(2)}) collective-permute-start(bf16[1536,128]{1,0:T(8,128)(2,1)S(1)} %collective-permute-done.5.refs_8_), channel_id=1, source_target_pairs={{0,8},{4,12},{8,0},{12,4},{16,24},{20,28},{24,16},{28,20},{1,9},{5... | collective-permute-start | bytes 1179656 | tf_op jit(solution)/shard_map/ppermute | solution.py:309
  94.6 31.7 %collective-permute-start.6 = (bf16[8,240,128]{2,1,0:T(8,128)(2,1)S(1)}, bf16[8,240,128]{2,1,0:T(8,128)(2,1)S(1)}, u32[]{:S(2)}, u32[]{:S(2)}) collective-permute-start(bf16[8,240,128]{2,1,0:T(8,128)(2,1)S(1)} %slice.4.refs_0_), channel_id=1, source_target_pairs={{0,1},{1,0},{2,3},{3,2},{4,5},{5,4},{6,7},{7,6},{8,9},{9,8},{10,11... | collective-permute-start | bytes 1474568 | tf_op jit(solution)/shard_map/ppermute | solution.py:309
  102.6 31.8 %collective-permute-start.8 = (bf16[8,240,128]{2,1,0:T(8,128)(2,1)S(1)}, bf16[8,240,128]{2,1,0:T(8,128)(2,1)S(1)}, u32[]{:S(2)}, u32[]{:S(2)}) collective-permute-start(bf16[8,240,128]{2,1,0:T(8,128)(2,1)S(1)} %collective-permute-done.7.refs_2_), channel_id=1, source_target_pairs={{0,1},{1,0},{2,3},{3,2},{4,5},{5,4},{6,7},{7,6},{8,9},{9,8},{10,11... | collective-permute-start | bytes 1474568 | tf_op jit(solution)/shard_map/ppermute | solution.py:309
  102.7 18.4 %collective-permute-start.9 = (bf16[1536,128]{1,0:T(8,128)(2,1)S(1)}, bf16[1536,128]{1,0:T(8,128)(2,1)S(1)}, u32[]{:S(2)}, u32[]{:S(2)}) collective-permute-start(bf16[1536,128]{1,0:T(8,128)(2,1)S(1)} %collective-permute-done.4.refs_6_), channel_id=1, source_target_pairs={{0,4},{4,0},{8,12},{12,8},{16,20},{20,16},{24,28},{28,24},{1,5},{5... | collective-permute-start | bytes 1179656 | tf_op jit(solution)/shard_map/ppermute | solution.py:309
  104.4 21.9 %collective-permute-start.10 = (bf16[1536,128]{1,0:T(8,128)(2,1)S(1)}, bf16[1536,128]{1,0:T(8,128)(2,1)S(1)}, u32[]{:S(2)}, u32[]{:S(2)}) collective-permute-start(bf16[1536,128]{1,0:T(8,128)(2,1)S(1)} %collective-permute-done.5.refs_8_), channel_id=1, source_target_pairs={{0,4},{4,0},{8,12},{12,8},{16,20},{20,16},{24,28},{28,24},{1,5},{5... | collective-permute-start | bytes 1179656 | tf_op jit(solution)/shard_map/ppermute | solution.py:309
  119.6 14.8 %collective-permute-start.12 = (bf16[1536,128]{1,0:T(8,128)(2,1)S(1)}, bf16[1536,128]{1,0:T(8,128)(2,1)S(1)}, u32[]{:S(2)}, u32[]{:S(2)}) collective-permute-start(bf16[1536,128]{1,0:T(8,128)(2,1)S(1)} %collective-permute-done.11.refs_10_), channel_id=1, source_target_pairs={{0,4},{4,0},{8,12},{12,8},{16,20},{20,16},{24,28},{28,24},{1,5},{5... | collective-permute-start | bytes 1179656 | tf_op jit(solution)/shard_map/ppermute | solution.py:309
  (8 other events, 6.8 us)
